TPU v7x, 256 devices: a whole 4x4x8 slice. The times are simulated.
256 devices in a mesh: slab: 4 (over x), row: 32 (over z, y), col: 2 (over core).
Axes of the slice: x: 4, y: 4, z: 8, core: 2. Of those that a mesh axis runs over, the one named last changes fastest.
Arguments:
- diagonals: bfloat16 [4, 1024, 1024], P('slab', 'row', 'col'), as said below
- lower_neighbour_coupling: bfloat16 [4, 1024, 1024], P('slab', 'row', 'col'), as said below
- upper_neighbour_coupling: bfloat16 [4, 1024, 1024], P('slab', 'row', 'col'), as said below
- right_hand_columns: bfloat16 [4, 1024, 512], P('slab', 'row', 'col'), may hold values from -6 to 6
Outputs:
- diag_out: bfloat16 [4, 1024, 1024], P('slab', 'row', 'col')
- lower_out: bfloat16 [4, 1024, 1024], P('slab', 'row', 'col')
- upper_out: bfloat16 [4, 1024, 1024], P('slab', 'row', 'col')
- sides_out: bfloat16 [4, 1024, 512], P('slab', 'row', 'col')
Inputs may be any that keep to these rules, and one draw needn't show every extreme that they name: Each slab's diagonal block has its diagonal in 1 to 2 and small independent entries off it, so that the pivots of all levels are dominated by their diagonals. `lower_neighbour_coupling`: independent entries of magnitude near 0.2 / sqrt(1024). `upper_neighbour_coupling`: independent entries of magnitude near 0.2 / sqrt(1024).
All inputs are finite; a program needn't handle non-finite values.
Results may differ from a plain program's by a relative error of at most 0.0075.
Values may be sent and summed in bfloat16 or wider, within the bound.
A program may use at most 64 MiB of HBM per device.

v0:
```python
import jax
import jax.numpy as jnp
from jax import lax
from jax.sharding import Mesh
from jax.sharding import PartitionSpec as P

SWEEPS = 2
ROW = ("row_0", "row_1")


def passed_along(block, axis, distance):
    devices = range(lax.axis_size(axis))
    route = [(i - distance, i) for i in devices if i - distance in devices]
    return lax.ppermute(block, axis, route)


def from_everyone(array, axis):
    size = lax.axis_size(axis)
    return lax.all_to_all(
        jnp.broadcast_to(array[None], (size, *array.shape)), axis, 0, 0, tiled=True
    )


def joined_along(parts, dim):
    shape = list(parts.shape[1:])
    shape[dim] *= parts.shape[0]
    return jnp.moveaxis(parts, 0, dim).reshape(shape)


def collect(array, axis, dim):
    parts = from_everyone(array, axis)
    return joined_along(parts, dim)


def gather_axes(array, axes, dim):
    if not axes:
        return array
    nearer = lax.all_gather(array, axes[-1], axis=dim, tiled=True)
    return gather_axes(nearer, axes[:-1], dim)


def per_device(diagonals, lower_neighbour_coupling, upper_neighbour_coupling, right_hand_columns):
    pivot_local_block = diagonals[0]
    lower_local_block = lower_neighbour_coupling[0]
    upper_local_block = upper_neighbour_coupling[0]
    sides_local_block = right_hand_columns[0]
    col_count = pivot_local_block.shape[1]
    slab_count = lax.axis_size("slab")
    slab_position = lax.axis_index("slab")
    col_index = lax.axis_index("col")
    lower_local_block = jnp.where(
        slab_position == 0, jnp.zeros_like(lower_local_block), lower_local_block
    )
    upper_local_block = jnp.where(
        slab_position == slab_count - 1, jnp.zeros_like(upper_local_block), upper_local_block
    )
    level_stride = 2**0
    from_after = passed_along(lower_local_block, "slab", -level_stride)
    from_before = passed_along(upper_local_block, "slab", level_stride)
    target = jnp.stack([from_after, from_before]).astype(jnp.float32)
    pivot_rows = collect(pivot_local_block, ROW, 0)
    square = lax.dynamic_slice_in_dim(pivot_rows, col_index * col_count, col_count, 0)
    divisor = jnp.diagonal(square).astype(jnp.float32)
    iterate = (target / divisor).astype(jnp.bfloat16)
    for sweep_index in range(SWEEPS):
        iterate_cols = collect(iterate, "col", 2)
        product = jnp.einsum(
            "akm,mn->akn", iterate_cols, pivot_rows, preferred_element_type=jnp.float32
        )
        iterate = (iterate.astype(jnp.float32) + (target - product) / divisor).astype(jnp.bfloat16)
    hand_sides = jnp.concatenate([upper_local_block, lower_local_block, sides_local_block], axis=1)
    factor_cols = collect(iterate, "col", 2)
    block_products = jnp.einsum(
        "akm,mn->akn",
        factor_cols,
        gather_axes(hand_sides, ROW, 0),
        preferred_element_type=jnp.float32,
    ).astype(jnp.bfloat16)
    update_before = passed_along(block_products[0], "slab", level_stride)
    update_after = passed_along(block_products[1], "slab", -level_stride)
    reduced_pivot = (
        pivot_local_block.astype(jnp.float32)
        - update_before[:, :col_count].astype(jnp.float32)
        - update_after[:, col_count : 2 * col_count].astype(jnp.float32)
    ).astype(jnp.bfloat16)
    reduced_sides = (
        sides_local_block.astype(jnp.float32)
        - update_before[:, 2 * col_count :].astype(jnp.float32)
        - update_after[:, 2 * col_count :].astype(jnp.float32)
    ).astype(jnp.bfloat16)
    lower_local_block = -update_before[:, col_count : 2 * col_count]
    upper_local_block = -update_after[:, :col_count]
    return (
        reduced_pivot[None],
        lower_local_block[None],
        upper_local_block[None],
        reduced_sides[None],
    )


def solution(mesh):
    torus = Mesh(
        mesh.devices.reshape(mesh.shape["slab"], 8, 4, mesh.shape["col"]),
        ("slab", "row_0", "row_1", "col"),
    )
    in_specs = (
        P("slab", ROW, "col"),
        P("slab", ROW, "col"),
        P("slab", ROW, "col"),
        P("slab", ROW, "col"),
    )
    out_specs = (
        P("slab", ROW, "col"),
        P("slab", ROW, "col"),
        P("slab", ROW, "col"),
        P("slab", ROW, "col"),
    )
    return jax.shard_map(
        per_device, mesh=torus, in_specs=in_specs, out_specs=out_specs, check_vma=False
    )
```

profile of v0, /device:TPU:1, one launch (start us, length us, event | category | flops | bytes accessed | tf_op | source)
XLA Modules:
  0.0 110.9 jit_solution(17798868850518950746)
XLA Ops:
  7.2 0.0 all-gather.2.cloned.1.call-start
  7.2 0.8 select_bitcast_fusion
  8.0 0.7 pad_maximum_fusion
  8.7 12.1 %all_gather.6 = bf16[128,1280]{1,0:T(8,128)(2,1)} all-gather(bf16[32,1280]{1,0:T(8,128)(2,1)S(1)} %pad_maximum_fusion), channel_id=1, replica_groups=mesh['slab'=4,'row_0'=8,'row_1'=4,'col'=2] {'row_1'}, dimensions={0}, use_global_device_ids=true | all-gather | bytes 409600 | tf_op jit(solution)/shard_map/all_gather | solution.py:38
  20.9 0.0 all-gather.2.cloned.1.call-update
  20.9 1.9 %broadcast_in_dim.20 = bf16[32,32,512]{2,1,0:T(8,128)(2,1)} broadcast(bf16[32,512]{1,0:T(8,128)(2,1)} %bitcast.55), dimensions={1,2} | broadcast | bytes 1081344 | tf_op jit(solution)/shard_map/broadcast_in_dim | solution.py:20
  22.8 9.9 %all-to-all-start = ((bf16[32,32,512]{2,1,0:T(8,128)(2,1)}), bf16[32,32,512]{2,1,0:T(8,128)(2,1)S(1)}, u32[]{:S(2)}, u32[]{:S(2)}) async-start(bf16[32,32,512]{2,1,0:T(8,128)(2,1)} %broadcast_in_dim.20), calls=%async_computation | async-start | bytes 2097152 | tf_op jit(solution)/shard_map/all_to_all | solution.py:19
  32.7 1.3 %collective-permute-start = (bf16[32,512]{1,0:T(8,128)(2,1)S(1)}, bf16[32,512]{1,0:T(8,128)(2,1)S(1)}, u32[]{:S(2)}, u32[]{:S(2)}) collective-permute-start(bf16[32,512]{1,0:T(8,128)(2,1)S(1)} %select_bitcast_fusion.1), channel_id=1, source_target_pairs={{64,0},{128,64},{192,128},{65,1},{129,65},{193,129},{66,2},{130,66... | collective-permute-start | bytes 98312 | tf_op jit(solution)/shard_map/ppermute | solution.py:14
  34.0 4.5 %collective-permute-start.1 = (bf16[32,512]{1,0:T(8,128)(2,1)S(1)}, bf16[32,512]{1,0:T(8,128)(2,1)S(1)}, u32[]{:S(2)}, u32[]{:S(2)}) collective-permute-start(bf16[32,512]{1,0:T(8,128)(2,1)S(1)} %select_bitcast_fusion), channel_id=1, source_target_pairs={{0,64},{64,128},{128,192},{1,65},{65,129},{129,193},{2,66},{66,130... | collective-permute-start | bytes 98312 | tf_op jit(solution)/shard_map/ppermute | solution.py:14
  38.5 23.7 %all-to-all-done = bf16[32,32,512]{2,1,0:T(8,128)(2,1)S(1)} async-done(((bf16[32,32,512]{2,1,0:T(8,128)(2,1)}), bf16[32,32,512]{2,1,0:T(8,128)(2,1)S(1)}, u32[]{:S(2)}, u32[]{:S(2)}) %all-to-all-start) | async-done | bytes 1048608 | tf_op jit(solution)/shard_map/all_to_all | solution.py:19
  62.3 4.8 %gather_fusion = bf16[512]{0:T(512)(128)(2,1)S(1)} fusion(bf16[512,512]{1,0:T(8,128)(2,1)S(1)} %constant_dynamic-slice_fusion, s32[512]{0:T(512)S(1)} %bitcast.45), kind=kCustom, calls=%fused_computation | custom fusion | bytes 6144 | tf_op jit(solution)/shard_map/jit(diagonal)/cond/branch_0_fun/gather | solution.py:63
  67.2 0.0 collective-permute-done
  67.2 0.0 collective-permute-done.1
  67.2 14.1 %all_to_all.20 = bf16[2,2,32,512]{3,2,1,0:T(8,128)(2,1)S(1)} all-to-all(bf16[2,2,32,512]{3,2,1,0:T(8,128)(2,1)S(1)} %broadcast_in_dim.21), channel_id=1, replica_groups=mesh['slab'=4,'row_0'=8,'row_1'=4,'col'=2] {'col'}, dimensions={0} | all-to-all | bytes 262144 | tf_op jit(solution)/shard_map/all_to_all | solution.py:19
  81.4 0.3 fusion.10
  81.7 3.8 %all_to_all.21 = bf16[2,2,32,512]{3,2,1,0:T(8,128)(2,1)S(1)} all-to-all(bf16[2,2,32,512]{3,2,1,0:T(8,128)(2,1)S(1)} %broadcast_in_dim.22), channel_id=1, replica_groups=mesh['slab'=4,'row_0'=8,'row_1'=4,'col'=2] {'col'}, dimensions={0} | all-to-all | bytes 262144 | tf_op jit(solution)/shard_map/all_to_all | solution.py:19
  85.5 0.3 fusion.9
  85.9 3.8 %all_to_all.22 = bf16[2,2,32,512]{3,2,1,0:T(8,128)(2,1)S(1)} all-to-all(bf16[2,2,32,512]{3,2,1,0:T(8,128)(2,1)S(1)} %broadcast_in_dim.23), channel_id=1, replica_groups=mesh['slab'=4,'row_0'=8,'row_1'=4,'col'=2] {'col'}, dimensions={0} | all-to-all | bytes 262144 | tf_op jit(solution)/shard_map/all_to_all | solution.py:19
  89.7 0.0 all-gather.2.cloned.1.call-done
  89.8 0.0 copy-start.1
  89.8 0.0 copy-start
  89.8 2.3 %fusion.2 = bf16[2,32,1280]{2,1,0:T(8,128)(2,1)S(1)} fusion(bf16[2,32,1024]{2,1,0:T(8,128)(2,1)S(1)} %bitcast.49, bf16[1024,1280]{1,0:T(8,128)(2,1)} %all-gather.2.cloned.1.call-done), kind=kOutput, calls=%fused_computation.3 | convolution fusion | flops 167854080 | bytes 2916352 | tf_op jit(solution)/shard_map/akm,mn->akn/dot_general | solution.py:73
  92.1 4.3 %collective-permute-start.2 = (bf16[32,1280]{1,0:T(8,128)(2,1)S(1)}, bf16[32,1280]{1,0:T(8,128)(2,1)S(1)}, u32[]{:S(2)}, u32[]{:S(2)}) collective-permute-start(bf16[32,1280]{1,0:T(8,128)(2,1)S(1)} %get-tuple-element.4), channel_id=1, source_target_pairs={{0,64},{64,128},{128,192},{1,65},{65,129},{129,193},{2,66},{66,130... | collective-permute-start | bytes 245768 | tf_op jit(solution)/shard_map/ppermute | solution.py:14
  96.4 1.3 %collective-permute-start.3 = (bf16[32,1280]{1,0:T(8,128)(2,1)S(1)}, bf16[32,1280]{1,0:T(8,128)(2,1)S(1)}, u32[]{:S(2)}, u32[]{:S(2)}) collective-permute-start(bf16[32,1280]{1,0:T(8,128)(2,1)S(1)} %get-tuple-element.5), channel_id=1, source_target_pairs={{64,0},{128,64},{192,128},{65,1},{129,65},{193,129},{66,2},{130,66... | collective-permute-start | bytes 245768 | tf_op jit(solution)/shard_map/ppermute | solution.py:14
  97.7 0.2 collective-permute-done.2
  97.9 3.7 %collective-permute-done.3 = bf16[32,1280]{1,0:T(8,128)(2,1)S(1)} collective-permute-done((bf16[32,1280]{1,0:T(8,128)(2,1)S(1)}, bf16[32,1280]{1,0:T(8,128)(2,1)S(1)}, u32[]{:S(2)}, u32[]{:S(2)}) %collective-permute-start.3) | collective-permute-done | bytes 81952 | tf_op jit(solution)/shard_map/ppermute | solution.py:14
  101.6 0.0 copy-done.1
  101.6 0.6 fusion.15
  102.2 0.0 copy-done
  102.2 0.6 fusion.12
  102.8 0.6 fusion.13
  103.5 0.6 fusion.14
  (12 shorter events, 0.2 us)
Async XLA Ops:
  7.2 82.6 %all-gather.2.cloned.1.call-start = ((), (), s32[]{:S(2)}) async-start(), calls=%async_computation.4 | async-start | bytes 2949120 | tf_op jit(solution)/shard_map/all_gather | solution.py:38
  22.8 39.5 %all-to-all-start = ((bf16[32,32,512]{2,1,0:T(8,128)(2,1)}), bf16[32,32,512]{2,1,0:T(8,128)(2,1)S(1)}, u32[]{:S(2)}, u32[]{:S(2)}) async-start(bf16[32,32,512]{2,1,0:T(8,128)(2,1)} %broadcast_in_dim.20), calls=%async_computation | async-start | bytes 2097152 | tf_op jit(solution)/shard_map/all_to_all | solution.py:19
  32.7 34.4 %collective-permute-start = (bf16[32,512]{1,0:T(8,128)(2,1)S(1)}, bf16[32,512]{1,0:T(8,128)(2,1)S(1)}, u32[]{:S(2)}, u32[]{:S(2)}) collective-permute-start(bf16[32,512]{1,0:T(8,128)(2,1)S(1)} %select_bitcast_fusion.1), channel_id=1, source_target_pairs={{64,0},{128,64},{192,128},{65,1},{129,65},{193,129},{66,2},{130,66... | collective-permute-start | bytes 98312 | tf_op jit(solution)/shard_map/ppermute | solution.py:14
  34.0 33.1 %collective-permute-start.1 = (bf16[32,512]{1,0:T(8,128)(2,1)S(1)}, bf16[32,512]{1,0:T(8,128)(2,1)S(1)}, u32[]{:S(2)}, u32[]{:S(2)}) collective-permute-start(bf16[32,512]{1,0:T(8,128)(2,1)S(1)} %select_bitcast_fusion), channel_id=1, source_target_pairs={{0,64},{64,128},{128,192},{1,65},{65,129},{129,193},{2,66},{66,130... | collective-permute-start | bytes 98312 | tf_op jit(solution)/shard_map/ppermute | solution.py:14
  89.8 11.8 %copy-start.1 = (bf16[1,32,256]{2,1,0:T(8,128)(2,1)S(1)}, bf16[1,32,256]{2,1,0:T(8,128)(2,1)}, u32[]{:S(2)}) copy-start(bf16[1,32,256]{2,1,0:T(8,128)(2,1)} %param.7) | copy-start | bytes 49156
  89.8 12.5 %copy-start = (bf16[1,32,512]{2,1,0:T(8,128)(2,1)S(1)}, bf16[1,32,512]{2,1,0:T(8,128)(2,1)}, u32[]{:S(2)}) copy-start(bf16[1,32,512]{2,1,0:T(8,128)(2,1)} %param.4) | copy-start | bytes 98308
  92.1 5.8 %collective-permute-start.2 = (bf16[32,1280]{1,0:T(8,128)(2,1)S(1)}, bf16[32,1280]{1,0:T(8,128)(2,1)S(1)}, u32[]{:S(2)}, u32[]{:S(2)}) collective-permute-start(bf16[32,1280]{1,0:T(8,128)(2,1)S(1)} %get-tuple-element.4), channel_id=1, source_target_pairs={{0,64},{64,128},{128,192},{1,65},{65,129},{129,193},{2,66},{66,130... | collective-permute-start | bytes 245768 | tf_op jit(solution)/shard_map/ppermute | solution.py:14
  96.4 5.2 %collective-permute-start.3 = (bf16[32,1280]{1,0:T(8,128)(2,1)S(1)}, bf16[32,1280]{1,0:T(8,128)(2,1)S(1)}, u32[]{:S(2)}, u32[]{:S(2)}) collective-permute-start(bf16[32,1280]{1,0:T(8,128)(2,1)S(1)} %get-tuple-element.5), channel_id=1, source_target_pairs={{64,0},{128,64},{192,128},{65,1},{129,65},{193,129},{66,2},{130,66... | collective-permute-start | bytes 245768 | tf_op jit(solution)/shard_map/ppermute | solution.py:14
Sparse Core Ops, SparseCore 0:
  21.0 62.8 all-gather.1
where the time goes:
time: 112 us; the launch traced here: 111 us
  blocking collectives  33.9 us (30%)
  waiting for transfers between devices  27.6 us (25%)
  starting transfers between devices  21.3 us (19%)
  between operations  14.2 us (13%)
  local copies, waits for them, and re-layouts  6.85 us (6%)
  other arithmetic  4.02 us (4%)
  matrix products  2.92 us (3%)
    all_to_all x1, waiting for transfers between devices, from_everyone(): lax.all_to_all(jnp.broadcast_to(array[None], (size, *array.shape)), axis,...  23.7 us
    all_to_all x3, blocking collectives, from_everyone(): lax.all_to_all(jnp.broadcast_to(array[None], (size, *array.shape)), axis,...  21.8 us
    all_gather x1, blocking collectives, gather_axes(): nearer = lax.all_gather(array, axes[-1], axis=dim, tiled=True)  12.1 us
    ppermute x4, starting transfers between devices, passed_along(): return lax.ppermute(block, axis, route)  11.4 us
    all_to_all x1, starting transfers between devices, from_everyone(): lax.all_to_all(jnp.broadcast_to(array[None], (size, *array.shape)), axis,...  9.94 us
    gather x1, local copies, waits for them, and re-layouts, per_device(): divisor = jnp.diagonal(square).astype(jnp.float32)  4.85 us
    ppermute x4, waiting for transfers between devices, passed_along(): return lax.ppermute(block, axis, route)  3.89 us
    dot_general x1, matrix products, per_device(): jnp.einsum('akm,mn->akn', factor_cols, gather_axes(hand_sides, ROW, 0), p...  2.31 us
  transfers between devices with their start and end apart: 6, of which 3 were waited for; matrix products, arithmetic and copies ran while one was open for 7% of the time, Pallas kernels for 0%

commit v1 on v0

v1 whole, which is shorter than its diff:
```python
import functools

import jax
import jax.numpy as jnp
from jax import lax
from jax.experimental import pallas as pl
from jax.experimental.pallas import tpu as pltpu
from jax.sharding import PartitionSpec as P

MESH = pl.DeviceIdType.MESH
SWEEPS = 2
SLABS, ZS, YS, CORES = 4, 8, 4, 2
ROWS = 32
HALF = 512
TILE = 128
BAND = YS * ROWS
PACKED = BAND + ROWS
NEAR_FIRST = (1, 7, 2, 6, 3, 5, 4)
FAR_FIRST = (4, 3, 5, 2, 6, 1, 7)


def kernel(
    pivot_in, lower_in, upper_in, sides_in,
    pivot_out, lower_out, upper_out, sides_out,
    pivot_own, lower_own, upper_own, sides_own,
    pivot, stacked, sides_raw, hand, sides_full, iterate, product, update,
    load_sem, z_send, z_recv, y_send, y_recv, core_send, core_recv,
    stack_send, stack_recv, pass_send, pass_recv, deal_send, deal_recv,
    ring_send, ring_recv, back_send, back_recv,
):
    x = lax.axis_index("slab")
    row = lax.axis_index("row")
    z, y = row // YS, row % YS
    c = lax.axis_index("col")

    def at(dx=0, dz=0, dy=0, dc=0):
        there = lax.rem(z + dz, ZS) * YS + lax.rem(y + dy, YS)
        return (lax.rem(x + dx, SLABS), there, lax.rem(c + dc, CORES))

    def remote(src, dst, send, recv, where):
        return pltpu.make_async_remote_copy(
            src_ref=src, dst_ref=dst, send_sem=send, recv_sem=recv,
            device_id=where, device_id_type=MESH,
        )

    def lanes(block, width=TILE):
        return pl.ds(pl.multiple_of(block * width, TILE), width)

    def band_rows(piece):
        return pl.ds(pl.multiple_of(piece * ROWS, ROWS), ROWS)

    loads = [
        pltpu.make_async_copy(pivot_in, pivot.at[c, z, y], load_sem.at[0]),
        pltpu.make_async_copy(upper_in, upper_own, load_sem.at[1]),
        pltpu.make_async_copy(lower_in, lower_own, load_sem.at[2]),
        pltpu.make_async_copy(sides_in, sides_own, load_sem.at[3]),
        pltpu.make_async_copy(upper_in.at[:, lanes(y)], hand.at[z, band_rows(y), pl.ds(0, TILE)], load_sem.at[4]),
        pltpu.make_async_copy(lower_in.at[:, lanes(y)], hand.at[z, band_rows(y), pl.ds(TILE, TILE)], load_sem.at[5]),
        pltpu.make_async_copy(sides_in.at[:, lanes(y // 2)], sides_raw.at[y], load_sem.at[6]),
        pltpu.make_async_copy(pivot_in, pivot_own, load_sem.at[7]),
    ]
    for load in loads:
        load.start()
    partners = [at(dz=d) for d in range(1, ZS)] + [at(dy=d) for d in range(1, YS)] + [at(dc=1)]
    partners += [at(dx=dx, dy=dy) for dx in (1, 3) for dy in range(YS)]
    barrier = pltpu.get_barrier_semaphore()
    for partner in partners:
        pl.semaphore_signal(barrier, inc=1, device_id=partner, device_id_type=MESH)
    for load in loads:
        load.wait()
    pl.semaphore_wait(barrier, len(partners))

    def z_copy(d):
        mine = pivot.at[c, z, y]
        return remote(mine, mine, z_send.at[d], z_recv.at[d], at(dz=d))

    def y_copy(d, dy):
        zs = lax.rem(z + ZS - d, ZS)
        mine = pivot.at[c, zs, y]
        return remote(mine, mine, y_send.at[d, dy], y_recv.at[d, dy], at(dy=dy))

    def core_copy(d, dy):
        zs, ys = lax.rem(z + ZS - d, ZS), lax.rem(y + YS - dy, YS)
        mine = pivot.at[c, zs, ys]
        return remote(mine, mine, core_send, core_recv, at(dc=1))

    def deal_copies(dy):
        to = lax.rem(y + dy, YS)
        rows = band_rows(y)
        where = at(dy=dy)
        return [
            remote(upper_own.at[:, lanes(to)], hand.at[z, rows, pl.ds(0, TILE)], deal_send.at[dy, 0], deal_recv.at[dy, 0], where),
            remote(lower_own.at[:, lanes(to)], hand.at[z, rows, pl.ds(TILE, TILE)], deal_send.at[dy, 1], deal_recv.at[dy, 1], where),
            remote(sides_own.at[:, lanes(to // 2)], sides_raw.at[y], deal_send.at[dy, 2], deal_recv.at[dy, 2], where),
        ]

    def stack_copies(dy):
        return [
            remote(lower_own, stacked.at[0, c, y], stack_send.at[0, dy], stack_recv.at[0, dy], at(dx=3, dy=dy)),
            remote(upper_own, stacked.at[1, c, y], stack_send.at[1, dy], stack_recv.at[1, dy], at(dx=1, dy=dy)),
        ]

    def pass_copies():
        return [
            remote(stacked.at[a, c], stacked.at[a, c], pass_send.at[a], pass_recv.at[a], at(dc=1))
            for a in range(2)
        ]

    def ring_copy(way, step, part):
        zs = lax.rem(z + (ZS - step if way == 0 else step), ZS)
        rows = hand.at[zs, pl.ds(part * (PACKED // 2), PACKED // 2)]
        return remote(rows, rows, ring_send.at[way, step, part], ring_recv.at[way, step, part], at(dz=1 if way == 0 else ZS - 1))

    def ring_parts(way, step):
        return (0, 1) if step < 3 else (way,)

    for d in FAR_FIRST:
        z_copy(d).start()
    for dy in (2, 1, 3):
        for copy in deal_copies(dy):
            copy.start()
    core_copy(0, 0).start()
    for dy in (2, 1, 3):
        y_copy(0, dy).start()
    for dy in range(YS):
        for copy in stack_copies(dy):
            copy.start()

    lane = lax.broadcasted_iota(jnp.int32, (ROWS, TILE), 1)
    left = lane < TILE // 2
    odd = lax.rem(y, 2) == 1

    for dy in range(1, YS):
        for copy in deal_copies(dy):
            copy.wait_recv()
    for t in range(2):
        low = sides_raw[2 * t].astype(jnp.float32)
        high = sides_raw[2 * t + 1].astype(jnp.float32)
        low = jnp.where(odd, pltpu.roll(low, TILE // 2, 1), low)
        high = jnp.where(odd, high, pltpu.roll(high, TILE // 2, 1))
        hand[z, BAND:PACKED, t * TILE:(t + 1) * TILE] = jnp.where(left, low, high).astype(jnp.bfloat16)

    def ring_start(step):
        for part in range(2):
            for way in range(2):
                if part in ring_parts(way, step):
                    ring_copy(way, step, part).start()

    def ring_wait(step):
        for part in range(2):
            for way in range(2):
                if part in ring_parts(way, step):
                    ring_copy(way, step, part).wait_recv()

    def ring_on(step):
        for part in range(2):
            for way in range(2):
                if part in ring_parts(way, step):
                    ring_copy(way, step, part).wait_recv()
                if step < 3 and part in ring_parts(way, step + 1):
                    ring_copy(way, step + 1, part).start()

    def z_arrival(d):
        z_copy(d).wait_recv()
        for dy in (2, 1, 3):
            y_copy(d, dy).start()
        core_copy(d, 0).start()

    def y_arrival(d):
        for dy in (1, 3, 2):
            y_copy(d, dy).wait_recv()
            core_copy(d, dy).start()

    ring_start(0)
    for d in (1, 7, 2, 6):
        z_arrival(d)
    ring_on(0)
    y_arrival(0)
    for d in (3, 5, 4):
        z_arrival(d)
    y_arrival(1)
    y_arrival(7)
    ring_on(1)
    for dy in range(YS):
        for copy in stack_copies(dy):
            copy.wait_recv()
    for copy in pass_copies():
        copy.start()
    y_arrival(2)
    y_arrival(6)
    ring_on(2)
    for d in (3, 5, 4):
        y_arrival(d)

    for copy in pass_copies():
        copy.wait_recv()
    theirs = pivot.at[1 - c]
    remote(theirs, theirs, core_send, core_recv, at(dc=1)).wait_recv()

    eye = lax.broadcasted_iota(jnp.int32, (BAND, TILE), 0) == lax.broadcasted_iota(jnp.int32, (BAND, TILE), 1)

    def inverse_of(h):
        found = []
        for t in range(HALF // TILE):
            block = pivot[h, h * (ZS // 2) + t, :, :, t * TILE:(t + 1) * TILE].reshape(BAND, TILE)
            found.append(jnp.sum(jnp.where(eye, block.astype(jnp.float32), 0.0), axis=0, keepdims=True))
        return 1.0 / jnp.concatenate(found, axis=1)

    inverse = [inverse_of(h) for h in range(CORES)]
    present = [x < SLABS - 1, x > 0]

    def target(a, h):
        block = stacked[a, h].reshape(BAND, HALF).astype(jnp.float32)
        return jnp.where(present[a], block, 0.0)

    for a in range(2):
        for h in range(CORES):
            iterate[0, a * BAND:(a + 1) * BAND, h * HALF:(h + 1) * HALF] = (target(a, h) * inverse[h]).astype(jnp.bfloat16)
    for sweep in range(SWEEPS):
        now, later = sweep % 2, (sweep + 1) % 2
        for h in range(CORES):
            columns = slice(h * HALF, (h + 1) * HALF)
            product[...] = jnp.dot(iterate[now], pivot[h].reshape(ZS * BAND, HALF), preferred_element_type=jnp.float32)
            for a in range(2):
                rows = slice(a * BAND, (a + 1) * BAND)
                step = (target(a, h) - product[rows]) * inverse[h]
                iterate[later, rows, columns] = (iterate[now, rows, columns].astype(jnp.float32) + step).astype(jnp.bfloat16)

    ring_wait(3)
    for zs in range(ZS):
        for t in range(2):
            packed = hand[zs, BAND:PACKED, t * TILE:(t + 1) * TILE].astype(jnp.float32)
            turned = pltpu.roll(packed, TILE // 2, 1)
            sides_full[zs, 2 * t] = jnp.where(odd, turned, packed).astype(jnp.bfloat16)
            sides_full[zs, 2 * t + 1] = jnp.where(odd, packed, turned).astype(jnp.bfloat16)
    factor = iterate[SWEEPS % 2]
    coupled = jnp.dot(factor, hand[:, :BAND, :].reshape(ZS * BAND, 2 * TILE), preferred_element_type=jnp.float32)
    upper_part = jnp.where(present[0], coupled[:, :TILE], 0.0).astype(jnp.bfloat16)
    lower_part = jnp.where(present[1], coupled[:, TILE:], 0.0).astype(jnp.bfloat16)
    product[:, :TILE] = jnp.dot(factor, sides_full[...].reshape(ZS * BAND, TILE), preferred_element_type=jnp.float32)
    sides_part = product[:, :TILE].astype(jnp.bfloat16)
    for a in range(2):
        rows = slice(a * BAND, (a + 1) * BAND)
        update[0, a, :, :, 0:TILE] = upper_part[rows].reshape(YS, ROWS, TILE)
        update[0, a, :, :, TILE:2 * TILE] = lower_part[rows].reshape(YS, ROWS, TILE)
        update[0, a, :, :, 2 * TILE:] = sides_part[rows].reshape(YS, ROWS, TILE)

    def back_copy(a, dy):
        to = lax.rem(y + dy, YS)
        return remote(update.at[0, a, to], update.at[1, a, y], back_send.at[a, dy], back_recv.at[a, dy], at(dx=1 if a == 0 else 3, dy=dy))

    for dy in (2, 1, 3, 0):
        for a in range(2):
            back_copy(a, dy).start()
    for dy in range(YS):
        for a in range(2):
            back_copy(a, dy).wait_recv()

    for t in range(YS):
        columns = slice(t * TILE, (t + 1) * TILE)
        before, after = update[1, 0, t].astype(jnp.float32), update[1, 1, t].astype(jnp.float32)
        reduced = pivot_own[:, columns].astype(jnp.float32) - before[:, :TILE] - after[:, TILE:2 * TILE]
        pivot_out[:, columns] = reduced.astype(jnp.bfloat16)
        lower_out[:, columns] = (-before[:, TILE:2 * TILE]).astype(jnp.bfloat16)
        upper_out[:, columns] = (-after[:, :TILE]).astype(jnp.bfloat16)
    for t in range(2):
        columns = slice(t * TILE, (t + 1) * TILE)
        terms = [
            jnp.where(left, update[1, a, 2 * t, :, 2 * TILE:].astype(jnp.float32), update[1, a, 2 * t + 1, :, 2 * TILE:].astype(jnp.float32))
            for a in range(2)
        ]
        reduced = sides_own[:, columns].astype(jnp.float32) - terms[0] - terms[1]
        sides_out[:, columns] = reduced.astype(jnp.bfloat16)

    for d in FAR_FIRST:
        z_copy(d).wait_send()
    for dy in range(1, YS):
        for copy in deal_copies(dy):
            copy.wait_send()
        for d in range(ZS):
            y_copy(d, dy).wait_send()
    for dy in range(YS):
        for copy in stack_copies(dy):
            copy.wait_send()
        for a in range(2):
            back_copy(a, dy).wait_send()
    for copy in pass_copies():
        copy.wait_send()
    mine = pivot.at[c]
    remote(mine, mine, core_send, core_recv, at(dc=1)).wait_send()
    for step in range(4):
        for way in range(2):
            for part in ring_parts(way, step):
                ring_copy(way, step, part).wait_send()


def per_device(diagonals, lower, upper, sides):
    square = jax.ShapeDtypeStruct((ROWS, HALF), jnp.bfloat16)
    wide = jax.ShapeDtypeStruct((ROWS, HALF // 2), jnp.bfloat16)
    whole = pl.BlockSpec(memory_space=pltpu.VMEM)
    bf16 = jnp.bfloat16
    dma = pltpu.SemaphoreType.DMA
    outs = pl.pallas_call(
        kernel,
        out_shape=(square, square, square, wide),
        in_specs=[pl.BlockSpec(memory_space=pl.ANY)] * 4,
        out_specs=(whole,) * 4,
        scratch_shapes=[
            pltpu.VMEM((ROWS, HALF), bf16),
            pltpu.VMEM((ROWS, HALF), bf16),
            pltpu.VMEM((ROWS, HALF), bf16),
            pltpu.VMEM((ROWS, HALF // 2), bf16),
            pltpu.VMEM((CORES, ZS, YS, ROWS, HALF), bf16),
            pltpu.VMEM((2, CORES, YS, ROWS, HALF), bf16),
            pltpu.VMEM((YS, ROWS, TILE), bf16),
            pltpu.VMEM((ZS, PACKED, 2 * TILE), bf16),
            pltpu.VMEM((ZS, YS, ROWS, TILE), bf16),
            pltpu.VMEM((2, 2 * BAND, CORES * HALF), bf16),
            pltpu.VMEM((2 * BAND, HALF), jnp.float32),
            pltpu.VMEM((2, 2, YS, ROWS, 3 * TILE), bf16),
            dma((8,)),
            dma((ZS,)), dma((ZS,)),
            dma((ZS, YS)), dma((ZS, YS)),
            dma, dma,
            dma((2, YS)), dma((2, YS)),
            dma((2,)), dma((2,)),
            dma((YS, 3)), dma((YS, 3)),
            dma((2, 4, 2)), dma((2, 4, 2)),
            dma((2, YS)), dma((2, YS)),
        ],
        compiler_params=pltpu.CompilerParams(
            collective_id=0, has_side_effects=True, vmem_limit_bytes=32 * 2**20
        ),
    )(diagonals[0], lower[0], upper[0], sides[0])
    return tuple(out[None] for out in outs)


def solution(mesh):
    spec = P("slab", "row", "col")
    return jax.shard_map(
        per_device, mesh=mesh, in_specs=(spec,) * 4, out_specs=(spec,) * 4, check_vma=False
    )
```

time: 112 us -> 45.2 us (0.40)
  Pallas kernels: 0 us -> 38.8 us
  blocking collectives: 33.9 us -> 0 us
  waiting for transfers between devices: 27.6 us -> 0 us
  starting transfers between devices: 21.3 us -> 0 us
  between operations: 14.2 us -> 0.65 us
  other arithmetic: 4.02 us -> 0 us
  matrix products: 2.92 us -> 0 us
  local copies, waits for them, and re-layouts: 6.85 us -> 5.43 us
    pallas_call x0 -> x1, Pallas kernels: none -> 38.8 us  [per_device(): pl.pallas_call(kernel, out_shape=(square, square, square, wide), in_specs...]
    all_to_all x1 -> x0, waiting for transfers between devices: 23.7 us -> none  [from_everyone(): lax.all_to_all(jnp.broadcast_to(array[None], (size, *array.shape)), axis,...]
    all_to_all x3 -> x0, blocking collectives: 21.8 us -> none  [from_everyone(): lax.all_to_all(jnp.broadcast_to(array[None], (size, *array.shape)), axis,...]
    all_gather x1 -> x0, blocking collectives: 12.1 us -> none  [gather_axes(): nearer = lax.all_gather(array, axes[-1], axis=dim, tiled=True)]
    ppermute x4 -> x0, starting transfers between devices: 11.4 us -> none  [passed_along(): return lax.ppermute(block, axis, route)]
    all_to_all x1 -> x0, starting transfers between devices: 9.94 us -> none  [from_everyone(): lax.all_to_all(jnp.broadcast_to(array[None], (size, *array.shape)), axis,...]
    unnamed x4 -> x12, local copies, waits for them, and re-layouts: 0.01 us -> 5.43 us
    gather x1 -> x0, local copies, waits for them, and re-layouts: 4.85 us -> none  [per_device(): divisor = jnp.diagonal(square).astype(jnp.float32)]
  transfers between devices with their start and end apart: 6 -> 0, of which waited for: 3 -> 0; matrix products, arithmetic and copies ran while one was open for 7% -> 0% of each run, Pallas kernels for 0% -> 0%
where the time goes in v1:
time: 45.2 us; the launch traced here: 44.9 us
  Pallas kernels  38.8 us (86%)
  local copies, waits for them, and re-layouts  5.43 us (12%)
  between operations  0.65 us (1%)
    pallas_call x1, Pallas kernels, per_device(): pl.pallas_call(kernel, out_shape=(square, square, square, wide), in_specs...  38.8 us
    unnamed x12, local copies, waits for them, and re-layouts  5.43 us

profile of v1, /device:TPU:1, one launch (start us, length us, event | category | flops | bytes accessed | tf_op | source)
XLA Modules:
  0.0 44.9 jit_solution(392220331183054495)
XLA Ops:
  0.6 0.0 copy-start
  0.6 0.7 %copy-done = bf16[1,32,512]{2,1,0:T(8,128)(2,1)S(1)} copy-done((bf16[1,32,512]{2,1,0:T(8,128)(2,1)S(1)}, bf16[1,32,512]{2,1,0:T(8,128)(2,1)}, u32[]{:S(2)}) %copy-start) | copy-done | bytes 32792
  1.4 0.0 copy-start.1
  1.4 0.8 %copy-done.1 = bf16[1,32,512]{2,1,0:T(8,128)(2,1)S(1)} copy-done((bf16[1,32,512]{2,1,0:T(8,128)(2,1)S(1)}, bf16[1,32,512]{2,1,0:T(8,128)(2,1)}, u32[]{:S(2)}) %copy-start.1) | copy-done | bytes 32792
  2.1 0.0 copy-start.2
  2.2 0.8 %copy-done.2 = bf16[1,32,512]{2,1,0:T(8,128)(2,1)S(1)} copy-done((bf16[1,32,512]{2,1,0:T(8,128)(2,1)S(1)}, bf16[1,32,512]{2,1,0:T(8,128)(2,1)}, u32[]{:S(2)}) %copy-start.2) | copy-done | bytes 32792
  2.9 0.0 copy-start.3
  2.9 0.7 %copy-done.3 = bf16[1,32,256]{2,1,0:T(8,128)(2,1)S(1)} copy-done((bf16[1,32,256]{2,1,0:T(8,128)(2,1)S(1)}, bf16[1,32,256]{2,1,0:T(8,128)(2,1)}, u32[]{:S(2)}) %copy-start.3) | copy-done | bytes 16408
  3.6 38.8 %shard_map.75 = (bf16[32,512]{1,0:T(8,128)(2,1)S(1)}, bf16[32,512]{1,0:T(8,128)(2,1)S(1)}, bf16[32,512]{1,0:T(8,128)(2,1)S(1)}, bf16[32,256]{1,0:T(8,128)(2,1)S(1)}) custom-call(bf16[32,512]{1,0:T(8,128)(2,1)S(1)} %bitcast.8, bf16[32,512]{1,0:T(8,128)(2,1)S(1)} %bitcast.9, bf16[32,512]{1,0:T(8,128)(2,1)S(1)} %bitcast.10, bf16[32,256]{1,0:T(8,128)(2,1)S(1)} %bitcast.14), custom_call_target="tpu_custom_call" | custom-call | tf_op jit(solution)/shard_map/pallas_call | solution.py:303
  42.4 0.6 %copy.12 = bf16[1,32,512]{2,1,0:T(8,128)(2,1)} copy(bf16[1,32,512]{2,1,0:T(8,128)(2,1)S(1)} %bitcast.13) | data formatting | bytes 65536
  43.0 0.6 %copy.13 = bf16[1,32,512]{2,1,0:T(8,128)(2,1)} copy(bf16[1,32,512]{2,1,0:T(8,128)(2,1)S(1)} %bitcast.12) | data formatting | bytes 65536
  43.7 0.6 %copy.14 = bf16[1,32,512]{2,1,0:T(8,128)(2,1)} copy(bf16[1,32,512]{2,1,0:T(8,128)(2,1)S(1)} %bitcast.11) | data formatting | bytes 65536
  44.3 0.6 %copy.15 = bf16[1,32,256]{2,1,0:T(8,128)(2,1)} copy(bf16[1,32,256]{2,1,0:T(8,128)(2,1)S(1)} %bitcast.15) | data formatting | bytes 32768
Async XLA Ops:
  0.6 0.8 %copy-start = (bf16[1,32,512]{2,1,0:T(8,128)(2,1)S(1)}, bf16[1,32,512]{2,1,0:T(8,128)(2,1)}, u32[]{:S(2)}) copy-start(bf16[1,32,512]{2,1,0:T(8,128)(2,1)} %param.4) | copy-start | bytes 98308
  1.4 0.8 %copy-start.1 = (bf16[1,32,512]{2,1,0:T(8,128)(2,1)S(1)}, bf16[1,32,512]{2,1,0:T(8,128)(2,1)}, u32[]{:S(2)}) copy-start(bf16[1,32,512]{2,1,0:T(8,128)(2,1)} %param.5) | copy-start | bytes 98308
  2.1 0.8 %copy-start.2 = (bf16[1,32,512]{2,1,0:T(8,128)(2,1)S(1)}, bf16[1,32,512]{2,1,0:T(8,128)(2,1)}, u32[]{:S(2)}) copy-start(bf16[1,32,512]{2,1,0:T(8,128)(2,1)} %param.6) | copy-start | bytes 98308
  2.9 0.7 %copy-start.3 = (bf16[1,32,256]{2,1,0:T(8,128)(2,1)S(1)}, bf16[1,32,256]{2,1,0:T(8,128)(2,1)}, u32[]{:S(2)}) copy-start(bf16[1,32,256]{2,1,0:T(8,128)(2,1)} %param.7) | copy-start | bytes 49156

commit v2 on v1

--- a/solution.py
+++ b/solution.py
@@ -16,7 +16,6 @@
 BAND = YS * ROWS
 PACKED = BAND + ROWS
 NEAR_FIRST = (1, 7, 2, 6, 3, 5, 4)
-FAR_FIRST = (4, 3, 5, 2, 6, 1, 7)
 
 
 def kernel(
@@ -114,7 +113,7 @@
     def ring_parts(way, step):
         return (0, 1) if step < 3 else (way,)
 
-    for d in FAR_FIRST:
+    for d in NEAR_FIRST:
         z_copy(d).start()
     for dy in (2, 1, 3):
         for copy in deal_copies(dy):
@@ -272,7 +271,7 @@
         reduced = sides_own[:, columns].astype(jnp.float32) - terms[0] - terms[1]
         sides_out[:, columns] = reduced.astype(jnp.bfloat16)
 
-    for d in FAR_FIRST:
+    for d in NEAR_FIRST:
         z_copy(d).wait_send()
     for dy in range(1, YS):
         for copy in deal_copies(dy):
@@ -294,6 +293,11 @@
                 ring_copy(way, step, part).wait_send()
 
 
+def hand_out(*refs):
+    for src, dst in zip(refs[:4], refs[4:]):
+        dst[...] = src[...]
+
+
 def per_device(diagonals, lower, upper, sides):
     square = jax.ShapeDtypeStruct((ROWS, HALF), jnp.bfloat16)
     wide = jax.ShapeDtypeStruct((ROWS, HALF // 2), jnp.bfloat16)
@@ -303,7 +307,7 @@
     outs = pl.pallas_call(
         kernel,
         out_shape=(square, square, square, wide),
-        in_specs=[pl.BlockSpec(memory_space=pl.ANY)] * 4,
+        in_specs=[pl.BlockSpec(memory_space=pltpu.HBM)] * 4,
         out_specs=(whole,) * 4,
         scratch_shapes=[
             pltpu.VMEM((ROWS, HALF), bf16),
@@ -329,9 +333,16 @@
             dma((2, YS)), dma((2, YS)),
         ],
         compiler_params=pltpu.CompilerParams(
-            collective_id=0, has_side_effects=True, vmem_limit_bytes=32 * 2**20
+            collective_id=0, has_side_effects=True, vmem_limit_bytes=60 * 2**20
         ),
     )(diagonals[0], lower[0], upper[0], sides[0])
+    outs = pl.pallas_call(
+        hand_out,
+        out_shape=(square, square, square, wide),
+        in_specs=[whole] * 4,
+        out_specs=[whole] * 4,
+        compiler_params=pltpu.CompilerParams(vmem_limit_bytes=60 * 2**20),
+    )(*outs)
     return tuple(out[None] for out in outs)
 
 

time: 45.2 us -> 40.6 us (0.90)
  local copies, waits for them, and re-layouts: 5.43 us -> 0 us
  Pallas kernels: 38.8 us -> 39.8 us
    unnamed x12 -> x0, local copies, waits for them, and re-layouts: 5.43 us -> none
    pallas_call x0 -> x1, Pallas kernels: none -> 1.44 us  [per_device(): pl.pallas_call(hand_out, out_shape=(square, square, square, wide), in_spe...]
    pallas_call x1, Pallas kernels: 38.8 us -> 38.3 us  [per_device(): pl.pallas_call(kernel, out_shape=(square, square, square, wide), in_specs...]
where the time goes in v2:
time: 40.6 us; the launch traced here: 40.4 us
  Pallas kernels  39.8 us (98%)
  between operations  0.64 us (2%)
    pallas_call x1, Pallas kernels, per_device(): pl.pallas_call(kernel, out_shape=(square, square, square, wide), in_specs...  38.3 us
    pallas_call x1, Pallas kernels, per_device(): pl.pallas_call(hand_out, out_shape=(square, square, square, wide), in_spe...  1.44 us

profile of v2, /device:TPU:1, one launch (start us, length us, event | category | flops | bytes accessed | tf_op | source)
XLA Modules:
  0.0 40.4 jit_solution(732187229907153389)
XLA Ops:
  0.6 38.3 %shard_map.75 = (bf16[32,512]{1,0:T(8,128)(2,1)}, bf16[32,512]{1,0:T(8,128)(2,1)}, bf16[32,512]{1,0:T(8,128)(2,1)}, bf16[32,256]{1,0:T(8,128)(2,1)}) custom-call(bf16[32,512]{1,0:T(8,128)(2,1)} %bitcast.8, bf16[32,512]{1,0:T(8,128)(2,1)} %bitcast.9, bf16[32,512]{1,0:T(8,128)(2,1)} %bitcast.10, bf16[32,256]{1,0:T(8,128)(2,1)} %bitcast.11), custom_call_target="tpu_custom_call" | custom-call | tf_op jit(solution)/shard_map/pallas_call | solution.py:307
  39.0 1.4 %shard_map.76 = (bf16[32,512]{1,0:T(8,128)(2,1)}, bf16[32,512]{1,0:T(8,128)(2,1)}, bf16[32,512]{1,0:T(8,128)(2,1)}, bf16[32,256]{1,0:T(8,128)(2,1)}) custom-call(bf16[32,512]{1,0:T(8,128)(2,1)} %get-tuple-element.12.refs_0_, bf16[32,512]{1,0:T(8,128)(2,1)} %get-tuple-element.13.refs_1_, bf16[32,512]{1,0:T(8,128)(2,1)} %get-tuple-element.14.refs_2_, ...), custom_call_target="tpu_custom_call" | custom-call | tf_op jit(solution)/shard_map/pallas_call | solution.py:339

commit v3 on v2

--- a/solution.py
+++ b/solution.py
@@ -15,6 +15,8 @@
 TILE = 128
 BAND = YS * ROWS
 PACKED = BAND + ROWS
+Y_RELAYED = (0, 1, 7)
+Z_RELAYED = ()
 NEAR_FIRST = (1, 7, 2, 6, 3, 5, 4)
 
 
@@ -25,7 +27,7 @@
     pivot, stacked, sides_raw, hand, sides_full, iterate, product, update,
     load_sem, z_send, z_recv, y_send, y_recv, core_send, core_recv,
     stack_send, stack_recv, pass_send, pass_recv, deal_send, deal_recv,
-    ring_send, ring_recv, back_send, back_recv,
+    band_send, band_recv, back_send, back_recv,
 ):
     x = lax.axis_index("slab")
     row = lax.axis_index("row")
@@ -69,14 +71,28 @@
         load.wait()
     pl.semaphore_wait(barrier, len(partners))
 
+    halves = (pl.ds(0, ROWS // 2), pl.ds(ROWS // 2, ROWS // 2))
+
     def z_copy(d):
         mine = pivot.at[c, z, y]
         return remote(mine, mine, z_send.at[d], z_recv.at[d], at(dz=d))
+
+    def z_relay(d):
+        way = 2 if d in (3, 4) else ZS - 2
+        mine = pivot.at[c, lax.rem(z + ZS - way, ZS), y]
+        if d in (0, 4):
+            mine = mine.at[halves[d // 4]]
+        return remote(mine, mine, z_send.at[d], z_recv.at[d], at(dz={3: 1, 4: 2, 5: ZS - 1, 0: ZS - 2}[d]))
 
     def y_copy(d, dy):
         zs = lax.rem(z + ZS - d, ZS)
         mine = pivot.at[c, zs, y]
         return remote(mine, mine, y_send.at[d, dy], y_recv.at[d, dy], at(dy=dy))
+
+    def y_relay(d, dy):
+        zs, ys = lax.rem(z + ZS - d, ZS), lax.rem(y + YS - dy, YS)
+        piece = pivot.at[c, zs, ys].at[halves[dy // 2]]
+        return remote(piece, piece, y_send.at[d, dy // 2 * 2], y_recv.at[d, dy // 2 * 2], at(dy=dy))
 
     def core_copy(d, dy):
         zs, ys = lax.rem(z + ZS - d, ZS), lax.rem(y + YS - dy, YS)
@@ -105,21 +121,20 @@
             for a in range(2)
         ]
 
-    def ring_copy(way, step, part):
-        zs = lax.rem(z + (ZS - step if way == 0 else step), ZS)
+    def band_copy(d, part):
+        behind, ahead = {1: (0, 1), 7: (0, 7), 2: (0, 2), 6: (0, 6), 3: (2, 1), 5: (6, 7), 4: ((2, 2), (6, 6))[part]}[d]
+        zs = lax.rem(z + ZS - behind, ZS)
         rows = hand.at[zs, pl.ds(part * (PACKED // 2), PACKED // 2)]
-        return remote(rows, rows, ring_send.at[way, step, part], ring_recv.at[way, step, part], at(dz=1 if way == 0 else ZS - 1))
-
-    def ring_parts(way, step):
-        return (0, 1) if step < 3 else (way,)
-
-    for d in NEAR_FIRST:
-        z_copy(d).start()
+        return remote(rows, rows, band_send.at[d, part], band_recv.at[d, part], at(dz=ahead))
+
     for dy in (2, 1, 3):
         for copy in deal_copies(dy):
             copy.start()
+    for d in NEAR_FIRST:
+        if d not in Z_RELAYED:
+            z_copy(d).start()
     core_copy(0, 0).start()
-    for dy in (2, 1, 3):
+    for dy in (1, 3) if 0 in Y_RELAYED else (2, 1, 3):
         y_copy(0, dy).start()
     for dy in range(YS):
         for copy in stack_copies(dy):
@@ -139,47 +154,60 @@
         high = jnp.where(odd, high, pltpu.roll(high, TILE // 2, 1))
         hand[z, BAND:PACKED, t * TILE:(t + 1) * TILE] = jnp.where(left, low, high).astype(jnp.bfloat16)
 
-    def ring_start(step):
+    for d in (2, 6, 1, 7):
         for part in range(2):
-            for way in range(2):
-                if part in ring_parts(way, step):
-                    ring_copy(way, step, part).start()
-
-    def ring_wait(step):
+            band_copy(d, part).start()
+
+    def band_on():
         for part in range(2):
-            for way in range(2):
-                if part in ring_parts(way, step):
-                    ring_copy(way, step, part).wait_recv()
-
-    def ring_on(step):
-        for part in range(2):
-            for way in range(2):
-                if part in ring_parts(way, step):
-                    ring_copy(way, step, part).wait_recv()
-                if step < 3 and part in ring_parts(way, step + 1):
-                    ring_copy(way, step + 1, part).start()
+            for d, further in ((2, (3, 4)), (6, (5, 4))):
+                band_copy(d, part).wait_recv()
+                for on in further:
+                    if on != 4 or part == (d == 6):
+                        band_copy(on, part).start()
 
     def z_arrival(d):
-        z_copy(d).wait_recv()
-        for dy in (2, 1, 3):
+        if d in Z_RELAYED:
+            z_relay(d).wait_recv()
+            if d == 4:
+                z_relay(0).wait_recv()
+        else:
+            z_copy(d).wait_recv()
+        if d in (2, 6) and Z_RELAYED:
+            for further in ((3, 4) if d == 2 else (5, 0)):
+                z_relay(further).start()
+        for dy in (1, 3) if d in Y_RELAYED else (2, 1, 3):
             y_copy(d, dy).start()
         core_copy(d, 0).start()
 
     def y_arrival(d):
-        for dy in (1, 3, 2):
+        for dy in (1, 3):
             y_copy(d, dy).wait_recv()
+            if d in Y_RELAYED:
+                y_relay(d, dy).start()
             core_copy(d, dy).start()
-
-    ring_start(0)
-    for d in (1, 7, 2, 6):
-        z_arrival(d)
-    ring_on(0)
+        if d not in Y_RELAYED:
+            y_copy(d, 2).wait_recv()
+            core_copy(d, 2).start()
+
+    def y_last(d):
+        if d in Y_RELAYED:
+            y_relay(d, 1).wait_recv()
+            y_relay(d, 3).wait_recv()
+            core_copy(d, 2).start()
+
+    z_arrival(1)
+    z_arrival(7)
+    z_arrival(2)
+    z_arrival(6)
     y_arrival(0)
-    for d in (3, 5, 4):
-        z_arrival(d)
+    z_arrival(3)
+    z_arrival(5)
+    z_arrival(4)
+    band_on()
     y_arrival(1)
     y_arrival(7)
-    ring_on(1)
+    y_last(0)
     for dy in range(YS):
         for copy in stack_copies(dy):
             copy.wait_recv()
@@ -187,9 +215,16 @@
         copy.start()
     y_arrival(2)
     y_arrival(6)
-    ring_on(2)
-    for d in (3, 5, 4):
-        y_arrival(d)
+    y_last(1)
+    y_last(7)
+    y_arrival(3)
+    y_arrival(5)
+    y_arrival(4)
+    y_last(2)
+    y_last(6)
+    y_last(3)
+    y_last(5)
+    y_last(4)
 
     for copy in pass_copies():
         copy.wait_recv()
@@ -225,7 +260,9 @@
                 step = (target(a, h) - product[rows]) * inverse[h]
                 iterate[later, rows, columns] = (iterate[now, rows, columns].astype(jnp.float32) + step).astype(jnp.bfloat16)
 
-    ring_wait(3)
+    for d in (1, 7, 3, 5, 4):
+        for part in range(2):
+            band_copy(d, part).wait_recv()
     for zs in range(ZS):
         for t in range(2):
             packed = hand[zs, BAND:PACKED, t * TILE:(t + 1) * TILE].astype(jnp.float32)
@@ -272,12 +309,18 @@
         sides_out[:, columns] = reduced.astype(jnp.bfloat16)
 
     for d in NEAR_FIRST:
-        z_copy(d).wait_send()
+        if d not in Z_RELAYED:
+            z_copy(d).wait_send()
+    for d in (3, 5, 4, 0) if Z_RELAYED else ():
+        z_relay(d).wait_send()
     for dy in range(1, YS):
         for copy in deal_copies(dy):
             copy.wait_send()
         for d in range(ZS):
-            y_copy(d, dy).wait_send()
+            if d not in Y_RELAYED or dy != 2:
+                y_copy(d, dy).wait_send()
+            if d in Y_RELAYED and dy != 2:
+                y_relay(d, dy).wait_send()
     for dy in range(YS):
         for copy in stack_copies(dy):
             copy.wait_send()
@@ -287,15 +330,18 @@
         copy.wait_send()
     mine = pivot.at[c]
     remote(mine, mine, core_send, core_recv, at(dc=1)).wait_send()
-    for step in range(4):
-        for way in range(2):
-            for part in ring_parts(way, step):
-                ring_copy(way, step, part).wait_send()
+    for d in range(1, ZS):
+        for part in range(2):
+            band_copy(d, part).wait_send()
 
 
 def hand_out(*refs):
-    for src, dst in zip(refs[:4], refs[4:]):
-        dst[...] = src[...]
+    sources, results, sem = refs[:4], refs[4:8], refs[8]
+    copies = [pltpu.make_async_copy(src, dst, sem.at[i]) for i, (src, dst) in enumerate(zip(sources, results))]
+    for copy in copies:
+        copy.start()
+    for copy in copies:
+        copy.wait()
 
 
 def per_device(diagonals, lower, upper, sides):
@@ -329,19 +375,20 @@
             dma((2, YS)), dma((2, YS)),
             dma((2,)), dma((2,)),
             dma((YS, 3)), dma((YS, 3)),
-            dma((2, 4, 2)), dma((2, 4, 2)),
+            dma((ZS, 2)), dma((ZS, 2)),
             dma((2, YS)), dma((2, YS)),
         ],
         compiler_params=pltpu.CompilerParams(
-            collective_id=0, has_side_effects=True, vmem_limit_bytes=60 * 2**20
+            collective_id=0, has_side_effects=True, vmem_limit_bytes=55104 * 2**10
         ),
     )(diagonals[0], lower[0], upper[0], sides[0])
     outs = pl.pallas_call(
         hand_out,
         out_shape=(square, square, square, wide),
-        in_specs=[whole] * 4,
-        out_specs=[whole] * 4,
-        compiler_params=pltpu.CompilerParams(vmem_limit_bytes=60 * 2**20),
+        in_specs=[pl.BlockSpec(memory_space=pl.ANY)] * 4,
+        out_specs=[pl.BlockSpec(memory_space=pl.ANY)] * 4,
+        scratch_shapes=[dma((4,))],
+        compiler_params=pltpu.CompilerParams(vmem_limit_bytes=55104 * 2**10),
     )(*outs)
     return tuple(out[None] for out in outs)
 

time: 40.6 us -> 38.9 us (0.958)
  Pallas kernels: 39.8 us -> 37.3 us
  local copies, waits for them, and re-layouts: 0 us -> 0.71 us
    pallas_call x1, Pallas kernels: 38.3 us -> 36.7 us  [per_device(): pl.pallas_call(kernel, out_shape=(square, square, square, wide), in_specs...]
    pallas_call x1, Pallas kernels: 1.44 us -> 0.68 us  [per_device(): pl.pallas_call(hand_out, out_shape=(square, square, square, wide), in_spe...]
    unnamed x0 -> x2, local copies, waits for them, and re-layouts: none -> 0.71 us
where the time goes in v3:
time: 38.9 us; the launch traced here: 38.7 us
  Pallas kernels  37.3 us (96%)
  local copies, waits for them, and re-layouts  0.71 us (2%)
  between operations  0.65 us (2%)
    pallas_call x1, Pallas kernels, per_device(): pl.pallas_call(kernel, out_shape=(square, square, square, wide), in_specs...  36.7 us

profile of v3, /device:TPU:1, one launch (start us, length us, event | category | flops | bytes accessed | tf_op | source)
XLA Modules:
  0.0 38.7 jit_solution(2152147350843859470)
XLA Ops:
  0.6 0.0 copy-start
  0.6 0.7 %copy-done = bf16[1,32,256]{2,1,0:T(8,128)(2,1)S(1)} copy-done((bf16[1,32,256]{2,1,0:T(8,128)(2,1)S(1)}, bf16[1,32,256]{2,1,0:T(8,128)(2,1)}, u32[]{:S(2)}) %copy-start) | copy-done | bytes 16408
  1.4 36.7 %shard_map.75 = (bf16[32,512]{1,0:T(8,128)(2,1)S(1)}, bf16[32,512]{1,0:T(8,128)(2,1)S(1)}, bf16[32,512]{1,0:T(8,128)(2,1)S(1)}, bf16[32,256]{1,0:T(8,128)(2,1)S(1)}) custom-call(bf16[32,512]{1,0:T(8,128)(2,1)} %bitcast.9, bf16[32,512]{1,0:T(8,128)(2,1)} %bitcast.10, bf16[32,512]{1,0:T(8,128)(2,1)} %bitcast.11, bf16[32,256]{1,0:T(8,128)(2,1)S(1)} %bitcast.8), custom_call_target="tpu_custom_call" | custom-call | tf_op jit(solution)/shard_map/pallas_call | solution.py:353
  38.0 0.7 %shard_map.76 = (bf16[32,512]{1,0:T(8,128)(2,1)}, bf16[32,512]{1,0:T(8,128)(2,1)}, bf16[32,512]{1,0:T(8,128)(2,1)}, bf16[32,256]{1,0:T(8,128)(2,1)}) custom-call(bf16[32,512]{1,0:T(8,128)(2,1)S(1)} %get-tuple-element.12.refs_0_, bf16[32,512]{1,0:T(8,128)(2,1)S(1)} %get-tuple-element.13.refs_1_, bf16[32,512]{1,0:T(8,128)(2,1)S(1)} %get-tuple-element.14.refs_2_, ...), custom_call_target="tpu_custom_call" | custom-call | tf_op jit(solution)/shard_map/pallas_call | solution.py:385
Async XLA Ops:
  0.6 0.7 %copy-start = (bf16[1,32,256]{2,1,0:T(8,128)(2,1)S(1)}, bf16[1,32,256]{2,1,0:T(8,128)(2,1)}, u32[]{:S(2)}) copy-start(bf16[1,32,256]{2,1,0:T(8,128)(2,1)} %param.7) | copy-start | bytes 49156

commit v4 on v2

--- a/solution.py
+++ b/solution.py
@@ -25,7 +25,7 @@
     pivot, stacked, sides_raw, hand, sides_full, iterate, product, update,
     load_sem, z_send, z_recv, y_send, y_recv, core_send, core_recv,
     stack_send, stack_recv, pass_send, pass_recv, deal_send, deal_recv,
-    ring_send, ring_recv, back_send, back_recv,
+    band_send, band_recv, back_send, back_recv,
 ):
     x = lax.axis_index("slab")
     row = lax.axis_index("row")
@@ -69,18 +69,22 @@
         load.wait()
     pl.semaphore_wait(barrier, len(partners))
 
+    def sent(ref, sem):
+        remote(ref, ref, sem, core_recv, at(dc=1)).wait_send()
+
+    def arrived(ref, sem):
+        remote(ref, ref, core_send, sem, at(dc=1)).wait_recv()
+
     def z_copy(d):
         mine = pivot.at[c, z, y]
-        return remote(mine, mine, z_send.at[d], z_recv.at[d], at(dz=d))
+        return remote(mine, mine, z_send, z_recv.at[d], at(dz=d))
 
     def y_copy(d, dy):
-        zs = lax.rem(z + ZS - d, ZS)
-        mine = pivot.at[c, zs, y]
-        return remote(mine, mine, y_send.at[d, dy], y_recv.at[d, dy], at(dy=dy))
-
-    def core_copy(d, dy):
-        zs, ys = lax.rem(z + ZS - d, ZS), lax.rem(y + YS - dy, YS)
-        mine = pivot.at[c, zs, ys]
+        mine = pivot.at[c, lax.rem(z + ZS - d, ZS), y]
+        return remote(mine, mine, y_send, y_recv.at[d], at(dy=dy))
+
+    def core_copy(d):
+        mine = pivot.at[c, lax.rem(z + ZS - d, ZS)]
         return remote(mine, mine, core_send, core_recv, at(dc=1))
 
     def deal_copies(dy):
@@ -88,15 +92,15 @@
         rows = band_rows(y)
         where = at(dy=dy)
         return [
-            remote(upper_own.at[:, lanes(to)], hand.at[z, rows, pl.ds(0, TILE)], deal_send.at[dy, 0], deal_recv.at[dy, 0], where),
-            remote(lower_own.at[:, lanes(to)], hand.at[z, rows, pl.ds(TILE, TILE)], deal_send.at[dy, 1], deal_recv.at[dy, 1], where),
-            remote(sides_own.at[:, lanes(to // 2)], sides_raw.at[y], deal_send.at[dy, 2], deal_recv.at[dy, 2], where),
+            remote(upper_own.at[:, lanes(to)], hand.at[z, rows, pl.ds(0, TILE)], deal_send.at[0], deal_recv.at[0], where),
+            remote(lower_own.at[:, lanes(to)], hand.at[z, rows, pl.ds(TILE, TILE)], deal_send.at[1], deal_recv.at[1], where),
+            remote(sides_own.at[:, lanes(to // 2)], sides_raw.at[y], deal_send.at[2], deal_recv.at[2], where),
         ]
 
     def stack_copies(dy):
         return [
-            remote(lower_own, stacked.at[0, c, y], stack_send.at[0, dy], stack_recv.at[0, dy], at(dx=3, dy=dy)),
-            remote(upper_own, stacked.at[1, c, y], stack_send.at[1, dy], stack_recv.at[1, dy], at(dx=1, dy=dy)),
+            remote(lower_own, stacked.at[0, c, y], stack_send, stack_recv, at(dx=3, dy=dy)),
+            remote(upper_own, stacked.at[1, c, y], stack_send, stack_recv, at(dx=1, dy=dy)),
         ]
 
     def pass_copies():
@@ -105,20 +109,17 @@
             for a in range(2)
         ]
 
-    def ring_copy(way, step, part):
-        zs = lax.rem(z + (ZS - step if way == 0 else step), ZS)
-        rows = hand.at[zs, pl.ds(part * (PACKED // 2), PACKED // 2)]
-        return remote(rows, rows, ring_send.at[way, step, part], ring_recv.at[way, step, part], at(dz=1 if way == 0 else ZS - 1))
-
-    def ring_parts(way, step):
-        return (0, 1) if step < 3 else (way,)
-
-    for d in NEAR_FIRST:
-        z_copy(d).start()
+    def band_copy(d, part=None):
+        behind, ahead = {1: (0, 1), 7: (0, 7), 2: (0, 2), 6: (0, 6), 3: (2, 1), 5: (6, 7), 4: ((2, 2), (6, 6))[part or 0]}[d]
+        zs = lax.rem(z + ZS - behind, ZS)
+        rows = hand.at[zs] if part is None else hand.at[zs, pl.ds(part * (PACKED // 2), PACKED // 2)]
+        return remote(rows, rows, band_send, band_recv.at[d if d in (2, 6) else 0], at(dz=ahead))
+
     for dy in (2, 1, 3):
         for copy in deal_copies(dy):
             copy.start()
-    core_copy(0, 0).start()
+    for d in NEAR_FIRST:
+        z_copy(d).start()
     for dy in (2, 1, 3):
         y_copy(0, dy).start()
     for dy in range(YS):
@@ -129,9 +130,8 @@
     left = lane < TILE // 2
     odd = lax.rem(y, 2) == 1
 
-    for dy in range(1, YS):
-        for copy in deal_copies(dy):
-            copy.wait_recv()
+    for kind in range(3):
+        arrived(sides_raw.at[pl.ds(0, YS - 1)], deal_recv.at[kind])
     for t in range(2):
         low = sides_raw[2 * t].astype(jnp.float32)
         high = sides_raw[2 * t + 1].astype(jnp.float32)
@@ -139,62 +139,37 @@
         high = jnp.where(odd, high, pltpu.roll(high, TILE // 2, 1))
         hand[z, BAND:PACKED, t * TILE:(t + 1) * TILE] = jnp.where(left, low, high).astype(jnp.bfloat16)
 
-    def ring_start(step):
-        for part in range(2):
-            for way in range(2):
-                if part in ring_parts(way, step):
-                    ring_copy(way, step, part).start()
-
-    def ring_wait(step):
-        for part in range(2):
-            for way in range(2):
-                if part in ring_parts(way, step):
-                    ring_copy(way, step, part).wait_recv()
-
-    def ring_on(step):
-        for part in range(2):
-            for way in range(2):
-                if part in ring_parts(way, step):
-                    ring_copy(way, step, part).wait_recv()
-                if step < 3 and part in ring_parts(way, step + 1):
-                    ring_copy(way, step + 1, part).start()
+    for d in (2, 6, 1, 7):
+        band_copy(d).start()
 
     def z_arrival(d):
         z_copy(d).wait_recv()
         for dy in (2, 1, 3):
             y_copy(d, dy).start()
-        core_copy(d, 0).start()
 
     def y_arrival(d):
-        for dy in (1, 3, 2):
-            y_copy(d, dy).wait_recv()
-            core_copy(d, dy).start()
-
-    ring_start(0)
+        arrived(pivot.at[c, 0, pl.ds(0, YS - 1)], y_recv.at[d])
+        core_copy(d).start()
+
     for d in (1, 7, 2, 6):
         z_arrival(d)
-    ring_on(0)
     y_arrival(0)
     for d in (3, 5, 4):
         z_arrival(d)
     y_arrival(1)
     y_arrival(7)
-    ring_on(1)
-    for dy in range(YS):
-        for copy in stack_copies(dy):
-            copy.wait_recv()
+    for d, further, half in ((2, 3, 0), (6, 5, 1)):
+        band_copy(d).wait_recv()
+        band_copy(further).start()
+        band_copy(4, half).start()
+    arrived(stacked.at[:, c], stack_recv)
     for copy in pass_copies():
         copy.start()
-    y_arrival(2)
-    y_arrival(6)
-    ring_on(2)
-    for d in (3, 5, 4):
+    for d in (2, 6, 3, 5, 4):
         y_arrival(d)
-
     for copy in pass_copies():
         copy.wait_recv()
-    theirs = pivot.at[1 - c]
-    remote(theirs, theirs, core_send, core_recv, at(dc=1)).wait_recv()
+    arrived(pivot.at[1 - c], core_recv)
 
     eye = lax.broadcasted_iota(jnp.int32, (BAND, TILE), 0) == lax.broadcasted_iota(jnp.int32, (BAND, TILE), 1)
 
@@ -225,7 +200,7 @@
                 step = (target(a, h) - product[rows]) * inverse[h]
                 iterate[later, rows, columns] = (iterate[now, rows, columns].astype(jnp.float32) + step).astype(jnp.bfloat16)
 
-    ring_wait(3)
+    arrived(hand.at[pl.ds(0, 5)], band_recv.at[0])
     for zs in range(ZS):
         for t in range(2):
             packed = hand[zs, BAND:PACKED, t * TILE:(t + 1) * TILE].astype(jnp.float32)
@@ -246,14 +221,12 @@
 
     def back_copy(a, dy):
         to = lax.rem(y + dy, YS)
-        return remote(update.at[0, a, to], update.at[1, a, y], back_send.at[a, dy], back_recv.at[a, dy], at(dx=1 if a == 0 else 3, dy=dy))
+        return remote(update.at[0, a, to], update.at[1, a, y], back_send, back_recv, at(dx=1 if a == 0 else 3, dy=dy))
 
     for dy in (2, 1, 3, 0):
         for a in range(2):
             back_copy(a, dy).start()
-    for dy in range(YS):
-        for a in range(2):
-            back_copy(a, dy).wait_recv()
+    arrived(update.at[1], back_recv)
 
     for t in range(YS):
         columns = slice(t * TILE, (t + 1) * TILE)
@@ -271,31 +244,25 @@
         reduced = sides_own[:, columns].astype(jnp.float32) - terms[0] - terms[1]
         sides_out[:, columns] = reduced.astype(jnp.bfloat16)
 
-    for d in NEAR_FIRST:
-        z_copy(d).wait_send()
-    for dy in range(1, YS):
-        for copy in deal_copies(dy):
-            copy.wait_send()
-        for d in range(ZS):
-            y_copy(d, dy).wait_send()
-    for dy in range(YS):
-        for copy in stack_copies(dy):
-            copy.wait_send()
-        for a in range(2):
-            back_copy(a, dy).wait_send()
+    sent(pivot.at[c, pl.ds(0, ZS - 1), 0], z_send)
+    sent(pivot.at[c, pl.ds(0, 6)], y_send)
+    sent(pivot.at[c], core_send)
+    sent(stacked.at[:, c], stack_send)
     for copy in pass_copies():
         copy.wait_send()
-    mine = pivot.at[c]
-    remote(mine, mine, core_send, core_recv, at(dc=1)).wait_send()
-    for step in range(4):
-        for way in range(2):
-            for part in ring_parts(way, step):
-                ring_copy(way, step, part).wait_send()
+    for kind in range(3):
+        sent(sides_raw.at[pl.ds(0, YS - 1)], deal_send.at[kind])
+    sent(hand.at[pl.ds(0, ZS - 1)], band_send)
+    sent(update.at[0], back_send)
 
 
 def hand_out(*refs):
-    for src, dst in zip(refs[:4], refs[4:]):
-        dst[...] = src[...]
+    sources, results, sem = refs[:4], refs[4:8], refs[8]
+    copies = [pltpu.make_async_copy(src, dst, sem.at[i]) for i, (src, dst) in enumerate(zip(sources, results))]
+    for copy in copies:
+        copy.start()
+    for copy in copies:
+        copy.wait()
 
 
 def per_device(diagonals, lower, upper, sides):
@@ -323,25 +290,26 @@
             pltpu.VMEM((2 * BAND, HALF), jnp.float32),
             pltpu.VMEM((2, 2, YS, ROWS, 3 * TILE), bf16),
             dma((8,)),
-            dma((ZS,)), dma((ZS,)),
-            dma((ZS, YS)), dma((ZS, YS)),
+            dma, dma((ZS,)),
+            dma, dma((ZS,)),
             dma, dma,
-            dma((2, YS)), dma((2, YS)),
+            dma, dma,
             dma((2,)), dma((2,)),
-            dma((YS, 3)), dma((YS, 3)),
-            dma((2, 4, 2)), dma((2, 4, 2)),
-            dma((2, YS)), dma((2, YS)),
+            dma((3,)), dma((3,)),
+            dma, dma((ZS,)),
+            dma, dma,
         ],
         compiler_params=pltpu.CompilerParams(
-            collective_id=0, has_side_effects=True, vmem_limit_bytes=60 * 2**20
+            collective_id=0, has_side_effects=True, vmem_limit_bytes=55104 * 2**10
         ),
-    )(diagonals[0], lower[0], upper[0], sides[0])
+    )(*(pltpu.with_memory_space_constraint(array[0], pltpu.HBM) for array in (diagonals, lower, upper, sides)))
     outs = pl.pallas_call(
         hand_out,
         out_shape=(square, square, square, wide),
-        in_specs=[whole] * 4,
-        out_specs=[whole] * 4,
-        compiler_params=pltpu.CompilerParams(vmem_limit_bytes=60 * 2**20),
+        in_specs=[pl.BlockSpec(memory_space=pl.ANY)] * 4,
+        out_specs=[pl.BlockSpec(memory_space=pl.ANY)] * 4,
+        scratch_shapes=[dma((4,))],
+        compiler_params=pltpu.CompilerParams(vmem_limit_bytes=55104 * 2**10),
     )(*outs)
     return tuple(out[None] for out in outs)
 

time: 40.6 us -> 37.1 us (0.914)
  Pallas kernels: 39.8 us -> 36.3 us
    pallas_call x1, Pallas kernels: 38.3 us -> 35.6 us  [per_device(): pl.pallas_call(kernel, out_shape=(square, square, square, wide), in_specs...]
    pallas_call x1, Pallas kernels: 1.44 us -> 0.68 us  [per_device(): pl.pallas_call(hand_out, out_shape=(square, square, square, wide), in_spe...]
where the time goes in v4:
time: 37.1 us; the launch traced here: 36.9 us
  Pallas kernels  36.3 us (98%)
  between operations  0.64 us (2%)
    pallas_call x1, Pallas kernels, per_device(): pl.pallas_call(kernel, out_shape=(square, square, square, wide), in_specs...  35.6 us

profile of v4, /device:TPU:1, one launch (start us, length us, event | category | flops | bytes accessed | tf_op | source)
XLA Modules:
  0.0 36.9 jit_solution(1487921308756998211)
XLA Ops:
  0.6 35.6 %shard_map.75 = (bf16[32,512]{1,0:T(8,128)(2,1)S(1)}, bf16[32,512]{1,0:T(8,128)(2,1)S(1)}, bf16[32,512]{1,0:T(8,128)(2,1)S(1)}, bf16[32,256]{1,0:T(8,128)(2,1)S(1)}) custom-call(bf16[32,512]{1,0:T(8,128)(2,1)} %bitcast.8, bf16[32,512]{1,0:T(8,128)(2,1)} %bitcast.9, bf16[32,512]{1,0:T(8,128)(2,1)} %bitcast.10, bf16[32,256]{1,0:T(8,128)(2,1)} %bitcast.11), custom_call_target="tpu_custom_call" | custom-call | tf_op jit(solution)/shard_map/pallas_call | solution.py:274
  36.2 0.7 %shard_map.76 = (bf16[32,512]{1,0:T(8,128)(2,1)}, bf16[32,512]{1,0:T(8,128)(2,1)}, bf16[32,512]{1,0:T(8,128)(2,1)}, bf16[32,256]{1,0:T(8,128)(2,1)}) custom-call(bf16[32,512]{1,0:T(8,128)(2,1)S(1)} %get-tuple-element.12.refs_0_, bf16[32,512]{1,0:T(8,128)(2,1)S(1)} %get-tuple-element.13.refs_1_, bf16[32,512]{1,0:T(8,128)(2,1)S(1)} %get-tuple-element.14.refs_2_, ...), custom_call_target="tpu_custom_call" | custom-call | tf_op jit(solution)/shard_map/pallas_call | solution.py:306

commit v5 on v4

--- a/solution.py
+++ b/solution.py
@@ -61,13 +61,27 @@
     for load in loads:
         load.start()
     partners = [at(dz=d) for d in range(1, ZS)] + [at(dy=d) for d in range(1, YS)] + [at(dc=1)]
-    partners += [at(dx=dx, dy=dy) for dx in (1, 3) for dy in range(YS)]
+    present = [x < SLABS - 1, x > 0]
     barrier = pltpu.get_barrier_semaphore()
     for partner in partners:
         pl.semaphore_signal(barrier, inc=1, device_id=partner, device_id_type=MESH)
+    for there, dx in zip(present, (1, SLABS - 1)):
+        @pl.when(there)
+        def greet(dx=dx):
+            for dy in range(YS):
+                pl.semaphore_signal(barrier, inc=1, device_id=at(dx=dx, dy=dy), device_id_type=MESH)
+
     for load in loads:
         load.wait()
-    pl.semaphore_wait(barrier, len(partners))
+    neighbours = present[0].astype(jnp.int32) + present[1].astype(jnp.int32)
+    pl.semaphore_wait(barrier, len(partners) + YS * neighbours)
+
+    for a in range(2):
+        @pl.when(jnp.logical_not(present[a]))
+        def no_stack(a=a):
+            stacked[a] = jnp.zeros(stacked.shape[1:], jnp.bfloat16)
+            update[1, 1 - a] = jnp.zeros(update.shape[2:], jnp.bfloat16)
+
 
     def sent(ref, sem):
         remote(ref, ref, sem, core_recv, at(dc=1)).wait_send()
@@ -97,17 +111,12 @@
             remote(sides_own.at[:, lanes(to // 2)], sides_raw.at[y], deal_send.at[2], deal_recv.at[2], where),
         ]
 
-    def stack_copies(dy):
-        return [
-            remote(lower_own, stacked.at[0, c, y], stack_send, stack_recv, at(dx=3, dy=dy)),
-            remote(upper_own, stacked.at[1, c, y], stack_send, stack_recv, at(dx=1, dy=dy)),
-        ]
-
-    def pass_copies():
-        return [
-            remote(stacked.at[a, c], stacked.at[a, c], pass_send.at[a], pass_recv.at[a], at(dc=1))
-            for a in range(2)
-        ]
+    def stack_copy(a, dy):
+        source, dx = ((lower_own, SLABS - 1), (upper_own, 1))[a]
+        return remote(source, stacked.at[a, c, y], stack_send.at[a], stack_recv.at[a], at(dx=dx, dy=dy))
+
+    def pass_copy(a):
+        return remote(stacked.at[a, c], stacked.at[a, c], pass_send.at[a], pass_recv.at[a], at(dc=1))
 
     def band_copy(d, part=None):
         behind, ahead = {1: (0, 1), 7: (0, 7), 2: (0, 2), 6: (0, 6), 3: (2, 1), 5: (6, 7), 4: ((2, 2), (6, 6))[part or 0]}[d]
@@ -122,9 +131,11 @@
         z_copy(d).start()
     for dy in (2, 1, 3):
         y_copy(0, dy).start()
-    for dy in range(YS):
-        for copy in stack_copies(dy):
-            copy.start()
+    for a in range(2):
+        @pl.when(present[1 - a])
+        def stack_start(a=a):
+            for dy in range(YS):
+                stack_copy(a, dy).start()
 
     lane = lax.broadcasted_iota(jnp.int32, (ROWS, TILE), 1)
     left = lane < TILE // 2
@@ -162,44 +173,16 @@
         band_copy(d).wait_recv()
         band_copy(further).start()
         band_copy(4, half).start()
-    arrived(stacked.at[:, c], stack_recv)
-    for copy in pass_copies():
-        copy.start()
-    for d in (2, 6, 3, 5, 4):
+    y_arrival(2)
+    y_arrival(6)
+    for a in range(2):
+        @pl.when(present[a])
+        def stack_on(a=a):
+            arrived(stacked.at[a, c], stack_recv.at[a])
+            pass_copy(a).start()
+
+    for d in (3, 5, 4):
         y_arrival(d)
-    for copy in pass_copies():
-        copy.wait_recv()
-    arrived(pivot.at[1 - c], core_recv)
-
-    eye = lax.broadcasted_iota(jnp.int32, (BAND, TILE), 0) == lax.broadcasted_iota(jnp.int32, (BAND, TILE), 1)
-
-    def inverse_of(h):
-        found = []
-        for t in range(HALF // TILE):
-            block = pivot[h, h * (ZS // 2) + t, :, :, t * TILE:(t + 1) * TILE].reshape(BAND, TILE)
-            found.append(jnp.sum(jnp.where(eye, block.astype(jnp.float32), 0.0), axis=0, keepdims=True))
-        return 1.0 / jnp.concatenate(found, axis=1)
-
-    inverse = [inverse_of(h) for h in range(CORES)]
-    present = [x < SLABS - 1, x > 0]
-
-    def target(a, h):
-        block = stacked[a, h].reshape(BAND, HALF).astype(jnp.float32)
-        return jnp.where(present[a], block, 0.0)
-
-    for a in range(2):
-        for h in range(CORES):
-            iterate[0, a * BAND:(a + 1) * BAND, h * HALF:(h + 1) * HALF] = (target(a, h) * inverse[h]).astype(jnp.bfloat16)
-    for sweep in range(SWEEPS):
-        now, later = sweep % 2, (sweep + 1) % 2
-        for h in range(CORES):
-            columns = slice(h * HALF, (h + 1) * HALF)
-            product[...] = jnp.dot(iterate[now], pivot[h].reshape(ZS * BAND, HALF), preferred_element_type=jnp.float32)
-            for a in range(2):
-                rows = slice(a * BAND, (a + 1) * BAND)
-                step = (target(a, h) - product[rows]) * inverse[h]
-                iterate[later, rows, columns] = (iterate[now, rows, columns].astype(jnp.float32) + step).astype(jnp.bfloat16)
-
     arrived(hand.at[pl.ds(0, 5)], band_recv.at[0])
     for zs in range(ZS):
         for t in range(2):
@@ -207,12 +190,45 @@
             turned = pltpu.roll(packed, TILE // 2, 1)
             sides_full[zs, 2 * t] = jnp.where(odd, turned, packed).astype(jnp.bfloat16)
             sides_full[zs, 2 * t + 1] = jnp.where(odd, packed, turned).astype(jnp.bfloat16)
+    for a in range(2):
+        @pl.when(present[a])
+        def passed(a=a):
+            pass_copy(a).wait_recv()
+
+    arrived(pivot.at[1 - c], core_recv)
+
+    eye = lax.broadcasted_iota(jnp.int32, (BAND, TILE), 0) == lax.broadcasted_iota(jnp.int32, (BAND, TILE), 1)
+
+    def inverse_of(h):
+        found = []
+        for t in range(HALF // TILE):
+            block = pivot[h, h * (ZS // 2) + t, :, :, t * TILE:(t + 1) * TILE].reshape(BAND, TILE)
+            found.append(jnp.sum(jnp.where(eye, block.astype(jnp.float32), 0.0), axis=0, keepdims=True))
+        return 1.0 / jnp.concatenate(found, axis=1)
+
+    inverse = [inverse_of(h) for h in range(CORES)]
+    def target(a, h):
+        block = stacked[a, h].reshape(BAND, HALF).astype(jnp.float32)
+        return jnp.where(present[a], block, 0.0)
+
+    for a in range(2):
+        for h in range(CORES):
+            iterate[0, a * BAND:(a + 1) * BAND, h * HALF:(h + 1) * HALF] = (target(a, h) * inverse[h]).astype(jnp.bfloat16)
+    for sweep in range(SWEEPS):
+        now, later = sweep % 2, (sweep + 1) % 2
+        for h in range(CORES):
+            columns = slice(h * HALF, (h + 1) * HALF)
+            for a in range(2):
+                rows = slice(a * BAND, (a + 1) * BAND)
+                moved = jnp.dot(iterate[now, rows], pivot[h].reshape(ZS * BAND, HALF), preferred_element_type=jnp.float32)
+                step = (target(a, h) - moved) * inverse[h]
+                iterate[later, rows, columns] = (iterate[now, rows, columns].astype(jnp.float32) + step).astype(jnp.bfloat16)
+
     factor = iterate[SWEEPS % 2]
     coupled = jnp.dot(factor, hand[:, :BAND, :].reshape(ZS * BAND, 2 * TILE), preferred_element_type=jnp.float32)
     upper_part = jnp.where(present[0], coupled[:, :TILE], 0.0).astype(jnp.bfloat16)
     lower_part = jnp.where(present[1], coupled[:, TILE:], 0.0).astype(jnp.bfloat16)
-    product[:, :TILE] = jnp.dot(factor, sides_full[...].reshape(ZS * BAND, TILE), preferred_element_type=jnp.float32)
-    sides_part = product[:, :TILE].astype(jnp.bfloat16)
+    sides_part = jnp.dot(factor, sides_full[...].reshape(ZS * BAND, TILE), preferred_element_type=jnp.float32).astype(jnp.bfloat16)
     for a in range(2):
         rows = slice(a * BAND, (a + 1) * BAND)
         update[0, a, :, :, 0:TILE] = upper_part[rows].reshape(YS, ROWS, TILE)
@@ -221,12 +237,18 @@
 
     def back_copy(a, dy):
         to = lax.rem(y + dy, YS)
-        return remote(update.at[0, a, to], update.at[1, a, y], back_send, back_recv, at(dx=1 if a == 0 else 3, dy=dy))
-
-    for dy in (2, 1, 3, 0):
-        for a in range(2):
-            back_copy(a, dy).start()
-    arrived(update.at[1], back_recv)
+        return remote(update.at[0, a, to], update.at[1, a, y], back_send.at[a], back_recv.at[a], at(dx=1 if a == 0 else 3, dy=dy))
+
+    for a in range(2):
+        @pl.when(present[a])
+        def back_start(a=a):
+            for dy in (2, 1, 3, 0):
+                back_copy(a, dy).start()
+
+    for a in range(2):
+        @pl.when(present[1 - a])
+        def back_arrival(a=a):
+            arrived(update.at[1, a], back_recv.at[a])
 
     for t in range(YS):
         columns = slice(t * TILE, (t + 1) * TILE)
@@ -247,13 +269,19 @@
     sent(pivot.at[c, pl.ds(0, ZS - 1), 0], z_send)
     sent(pivot.at[c, pl.ds(0, 6)], y_send)
     sent(pivot.at[c], core_send)
-    sent(stacked.at[:, c], stack_send)
-    for copy in pass_copies():
-        copy.wait_send()
+    for a in range(2):
+        @pl.when(present[1 - a])
+        def stack_sent(a=a):
+            sent(stacked.at[a, c], stack_send.at[a])
+
+        @pl.when(present[a])
+        def rest_sent(a=a):
+            pass_copy(a).wait_send()
+            sent(update.at[0, a], back_send.at[a])
+
     for kind in range(3):
         sent(sides_raw.at[pl.ds(0, YS - 1)], deal_send.at[kind])
     sent(hand.at[pl.ds(0, ZS - 1)], band_send)
-    sent(update.at[0], back_send)
 
 
 def hand_out(*refs):
@@ -293,11 +321,11 @@
             dma, dma((ZS,)),
             dma, dma((ZS,)),
             dma, dma,
-            dma, dma,
+            dma((2,)), dma((2,)),
             dma((2,)), dma((2,)),
             dma((3,)), dma((3,)),
             dma, dma((ZS,)),
-            dma, dma,
+            dma((2,)), dma((2,)),
         ],
         compiler_params=pltpu.CompilerParams(
             collective_id=0, has_side_effects=True, vmem_limit_bytes=55104 * 2**10

time: 37.1 us -> 36.2 us (0.976)
  Pallas kernels: 36.3 us -> 35.4 us
    pallas_call x1, Pallas kernels: 35.6 us -> 34.7 us  [per_device(): pl.pallas_call(kernel, out_shape=(square, square, square, wide), in_specs...]
where the time goes in v5:
time: 36.2 us; the launch traced here: 36 us
  Pallas kernels  35.4 us (98%)
  between operations  0.64 us (2%)
    pallas_call x1, Pallas kernels, per_device(): pl.pallas_call(kernel, out_shape=(square, square, square, wide), in_specs...  34.7 us

profile of v5, /device:TPU:1, one launch (start us, length us, event | category | flops | bytes accessed | tf_op | source)
XLA Modules:
  0.0 36.0 jit_solution(16041122473924207866)
XLA Ops:
  0.6 34.7 %shard_map.75 = (bf16[32,512]{1,0:T(8,128)(2,1)S(1)}, bf16[32,512]{1,0:T(8,128)(2,1)S(1)}, bf16[32,512]{1,0:T(8,128)(2,1)S(1)}, bf16[32,256]{1,0:T(8,128)(2,1)S(1)}) custom-call(bf16[32,512]{1,0:T(8,128)(2,1)} %bitcast.8, bf16[32,512]{1,0:T(8,128)(2,1)} %bitcast.9, bf16[32,512]{1,0:T(8,128)(2,1)} %bitcast.10, bf16[32,256]{1,0:T(8,128)(2,1)} %bitcast.11), custom_call_target="tpu_custom_call" | custom-call | tf_op jit(solution)/shard_map/pallas_call | solution.py:302
  35.3 0.7 %shard_map.76 = (bf16[32,512]{1,0:T(8,128)(2,1)}, bf16[32,512]{1,0:T(8,128)(2,1)}, bf16[32,512]{1,0:T(8,128)(2,1)}, bf16[32,256]{1,0:T(8,128)(2,1)}) custom-call(bf16[32,512]{1,0:T(8,128)(2,1)S(1)} %get-tuple-element.12.refs_0_, bf16[32,512]{1,0:T(8,128)(2,1)S(1)} %get-tuple-element.13.refs_1_, bf16[32,512]{1,0:T(8,128)(2,1)S(1)} %get-tuple-element.14.refs_2_, ...), custom_call_target="tpu_custom_call" | custom-call | tf_op jit(solution)/shard_map/pallas_call | solution.py:334
